TPU v7x, 512 devices: a whole 4x4x16 slice. The times are simulated.
512 devices in a mesh: row: 128 (over z, x, y_hi), gz: 4 (over y_lo, core).
Axes of the slice: x: 4, y: 4 (y_hi: 2, y_lo: 2; y = y_hi * 2 + y_lo), z: 16, core: 2. Of those that a mesh axis runs over, the one named last changes fastest.
Arguments:
- state: float32 [4, 1024, 16, 2048], P(None, 'row', 'gz'), may hold values from -12 to 12, as said below
- green: bfloat16 [128, 1024, 1024], P('row'), may hold values from -1 to 5
- vertical: float32 [16, 16], replicated, may hold values from 0 to 1
Outputs:
- new_state: float32 [4, 1024, 16, 2048], P(None, 'row', 'gz')
- potential: float32 [1024, 16, 2048], P('row', 'gz')
Inputs may be any that keep to these rules, and one draw needn't show every extreme that they name: `state`: component 0 lies in 0.25 to 4; components 1 and 2 are at most 3 times component 0 in magnitude; component 3 lies between 0 and component 0.
All inputs are finite; a program needn't handle non-finite values.
Results may differ from a plain program's by a relative error of at most 0.0019.
Values may be sent and summed in bfloat16 or wider, within the bound.
A program may use at most 64 MiB of HBM per device.

v0:
```python
import math

import jax
import jax.numpy as jnp
from jax import lax
from jax.sharding import Mesh
from jax.sharding import PartitionSpec as P

ROW = ("row_0", "row_1", "row_2")


sound_sq = 1.0
inner_radius = 1.0
radial_span = 4.0
courant = 0.2
precise = lax.Precision.HIGHEST


def padded_2(cells, sides, width):
    for axis, dim in sides:
        count = lax.axis_size(axis)
        ends = count - 1
        head = lax.slice_in_dim(cells, 0, width, axis=dim)
        tail = lax.slice_in_dim(cells, cells.shape[dim] - width, cells.shape[dim], axis=dim)
        cells = jnp.concatenate(
            [
                lax.ppermute(tail, axis, [(i, (i + 1) % count) for i in range(ends)]),
                cells,
                lax.ppermute(head, axis, [((i + 1) % count, i) for i in range(ends)]),
            ],
            axis=dim,
        )
    return cells


def cut_along(array, dim, peers):
    lengths = array.shape
    tiles = array.reshape(*lengths[:dim], peers, lengths[dim] // peers, *lengths[dim + 1 :])
    return jnp.moveaxis(tiles, dim, 0)


def in_order(tiles, dim):
    tiles = jnp.moveaxis(tiles, 0, dim)
    lengths = tiles.shape
    return tiles.reshape(*lengths[:dim], lengths[dim] * lengths[dim + 1], *lengths[dim + 2 :])


def moved_by_axis(tiles, axes, order):
    inside = tiles.shape[1:]
    result = tiles.reshape(*(lax.axis_size(a) for a in axes), *inside)
    for k in order:
        result = lax.all_to_all(result, axes[k], k, k, tiled=True)
    return result.reshape(-1, *inside)


def one_axis_at_a_time(array, axes, order, split_dim, concat_dim):
    tiles = cut_along(array, split_dim, lax.axis_size(axes))
    return in_order(moved_by_axis(tiles, axes, order), concat_dim)


def mode_table(azimuth, modes):
    angle_index = (
        jnp.arange(azimuth, dtype=jnp.int32)[:, None]
        * jnp.arange(modes, dtype=jnp.int32)[None, :]
        % azimuth
    )
    angles = angle_index.astype(jnp.float32) * (2.0 * math.pi / azimuth)
    forward = jnp.concatenate([jnp.cos(angles), -jnp.sin(angles)], axis=1)
    weights = jnp.where(jnp.arange(modes) == 0, 1.0, 2.0) / azimuth
    weights = jnp.concatenate([weights, weights]).astype(jnp.float32)
    inverse = forward.T * weights[:, None]
    return (forward, inverse)


def minmod(former, latter):
    return jnp.where(
        former * latter > 0, jnp.where(jnp.abs(former) < jnp.abs(latter), former, latter), 0.0
    )


def rusanov(left_state, right_state, normal):
    onehot = (jnp.arange(4) == normal).astype(left_state.dtype).reshape(4, 1, 1, 1)

    def flux_of(values):
        velocity = values[normal] / values[0]
        return (values * velocity + sound_sq * values[0] * onehot, jnp.abs(velocity))

    flux_left, speed_left = flux_of(left_state)
    flux_right, speed_right = flux_of(right_state)
    reach = jnp.maximum(speed_left, speed_right) + math.sqrt(sound_sq)
    return 0.5 * (flux_left + flux_right) - 0.5 * reach * (right_state - left_state)


def advance(padded, potential, radial_slope, centres, radial_step):
    azimuth = padded.shape[-1]
    phi_step = 2.0 * math.pi / azimuth
    step_time = courant * min(radial_step, inner_radius * phi_step)
    slopes = minmod(padded[:, 1:-1] - padded[:, :-2], padded[:, 2:] - padded[:, 1:-1])
    centre_cells = padded[:, 1:-1]
    flux_radial = rusanov(
        centre_cells[:, :-1] + 0.5 * slopes[:, :-1], centre_cells[:, 1:] - 0.5 * slopes[:, 1:], 1
    )
    interior = padded[:, 2:-2]
    phi_slopes = minmod(
        interior - jnp.roll(interior, 1, axis=3), jnp.roll(interior, -1, axis=3) - interior
    )
    flux_phi = rusanov(
        interior + 0.5 * phi_slopes, jnp.roll(interior - 0.5 * phi_slopes, -1, axis=3), 2
    )
    face_radii = jnp.concatenate(
        [centres - 0.5 * radial_step, centres[-1:] + 0.5 * radial_step]
    ).reshape(1, -1, 1, 1)
    weighted = face_radii * flux_radial
    radius = centres.reshape(1, -1, 1, 1)
    tendency = (
        -(
            (weighted[:, 1:] - weighted[:, :-1]) / radial_step
            + (flux_phi - jnp.roll(flux_phi, 1, axis=3)) / phi_step
        )
        / radius
    )
    density = interior[0]
    spin = interior[2] / density
    radius_cells = centres.reshape(-1, 1, 1)
    azimuth_slope = (jnp.roll(potential, -1, axis=2) - jnp.roll(potential, 1, axis=2)) / (
        2.0 * phi_step
    )
    force_radial = (interior[2] * spin + sound_sq * density) / radius_cells - density * radial_slope
    force_phi = -(interior[1] * spin + density * azimuth_slope) / radius_cells
    zeros = jnp.zeros_like(density)
    sources = jnp.stack([zeros, force_radial, force_phi, zeros])
    return interior + step_time * (tendency + sources)


def mend_edges(padded, width, axis_dim):
    length = padded.shape[axis_dim]
    position = lax.axis_index(ROW)
    last_rank = lax.axis_size(ROW) - 1
    low_rim = lax.slice_in_dim(padded, 0, width, axis=axis_dim)
    middle = lax.slice_in_dim(padded, width, length - width, axis=axis_dim)
    high_rim = lax.slice_in_dim(padded, length - width, length, axis=axis_dim)
    first_cell = lax.slice_in_dim(middle, 0, 1, axis=axis_dim)
    last_cell = lax.slice_in_dim(
        middle, middle.shape[axis_dim] - 1, middle.shape[axis_dim], axis=axis_dim
    )
    low_rim = jnp.where(position == 0, jnp.broadcast_to(first_cell, low_rim.shape), low_rim)
    high_rim = jnp.where(
        position == last_rank, jnp.broadcast_to(last_cell, high_rim.shape), high_rim
    )
    return jnp.concatenate([low_rim, middle, high_rim], axis=axis_dim)


def body(state, green, vertical):
    radii, planes, azimuth = (state.shape[1], state.shape[2], state.shape[3])
    modes_dev, radial_all = (green.shape[0], green.shape[1])
    modes = modes_dev * lax.axis_size(ROW)
    radial_step = radial_span / radial_all
    forward, inverse = mode_table(azimuth, modes)
    padded_state = mend_edges(padded_2(state, ((ROW, 1),), 2), 2, 1)
    spectrum = jnp.dot(
        state[0].reshape(-1, azimuth),
        forward,
        precision=precise,
        preferred_element_type=jnp.float32,
    ).reshape(radii, planes, 2, modes)
    plane_start = lax.axis_index("gz") * planes
    column_all = lax.all_gather(spectrum, "gz", axis=1, tiled=True)
    own_rows = lax.dynamic_slice_in_dim(vertical, plane_start, planes, 0)
    mixed = jnp.einsum("zy,ryck->rzck", own_rows, column_all, precision=precise)
    mixed_b = mixed.astype(jnp.bfloat16)
    pot_modes = jnp.einsum(
        "mrs,skcm->rkcm",
        green,
        lax.all_to_all(mixed_b, ROW, split_axis=3, concat_axis=0, tiled=True),
        preferred_element_type=jnp.float32,
    )
    pot_spec = one_axis_at_a_time(pot_modes, ROW, (0, 1, 2), 0, 3)
    potential = jnp.dot(
        pot_spec.reshape(-1, 2 * modes),
        inverse,
        precision=precise,
        preferred_element_type=jnp.float32,
    ).reshape(radii, planes, azimuth)
    padded_pot = mend_edges(padded_2(potential, ((ROW, 0),), 1), 1, 0)
    radial_slope = (padded_pot[2:] - padded_pot[:-2]) / (2.0 * radial_step)
    offsets = (lax.axis_index(ROW) * radii + jnp.arange(radii, dtype=jnp.int32)).astype(jnp.float32)
    centres = inner_radius + (offsets + 0.5) * radial_step
    new_state = advance(padded_state, potential, radial_slope, centres, radial_step)
    return (new_state, potential)


def solution(mesh):
    torus = Mesh(
        mesh.devices.reshape(16, 4, 2, mesh.shape["gz"]), ("row_0", "row_1", "row_2", "gz")
    )
    placed = (P(None, ROW, "gz", None), P(ROW, None, None), P())
    return jax.shard_map(
        body,
        mesh=torus,
        in_specs=placed,
        out_specs=(P(None, ROW, "gz", None), P(ROW, "gz", None)),
        check_vma=False,
    )
```

profile of v0, /device:TPU:32, one launch (start us, length us, event | category | flops | bytes accessed | tf_op | source)
XLA Modules:
  0.0 155.9 jit_solution(2098762484247323744)
XLA Ops:
  0.6 2.0 %fusion.57 = (f32[4,2,4,2048]{3,2,1,0:T(4,128)}, f32[4,2,4,2048]{3,2,1,0:T(4,128)}) fusion(f32[4,8,4,2048]{3,2,1,0:T(4,128)} %param.3), kind=kLoop, calls=%fused_computation.120 | loop fusion | bytes 1048576 | tf_op jit(solution)/shard_map/slice | solution.py:24
  2.7 5.1 %collective-permute-start = (f32[4,2,4,2048]{3,2,1,0:T(4,128)}, f32[4,2,4,2048]{3,2,1,0:T(4,128)}, u32[]{:S(2)}, u32[]{:S(2)}) collective-permute-start(f32[4,2,4,2048]{3,2,1,0:T(4,128)} %get-tuple-element.18), channel_id=1, source_target_pairs={{0,4},{4,8},{8,12},{12,16},{16,20},{20,24},{24,28},{28,32},{32,36}... | collective-permute-start | bytes 786440 | tf_op jit(solution)/shard_map/ppermute | solution.py:27
  7.8 5.3 %collective-permute-start.1 = (f32[4,2,4,2048]{3,2,1,0:T(4,128)}, f32[4,2,4,2048]{3,2,1,0:T(4,128)}, u32[]{:S(2)}, u32[]{:S(2)}) collective-permute-start(f32[4,2,4,2048]{3,2,1,0:T(4,128)} %get-tuple-element.19), channel_id=1, source_target_pairs={{4,0},{8,4},{12,8},{16,12},{20,16},{24,20},{28,24},{32,28},{36,32}... | collective-permute-start | bytes 786440 | tf_op jit(solution)/shard_map/ppermute | solution.py:29
  13.1 5.3 %sine_negate_fusion = (f32[2048,128]{1,0:T(8,128)S(1)}, f32[2048,128]{1,0:T(8,128)}) fusion(), kind=kLoop, calls=%fused_computation.50 | loop fusion | flops 3932160 | bytes 2097152 | tf_op jit(solution)/shard_map/neg | solution.py:68
  19.4 2.5 %fusion.11 = f32[32,256]{1,0:T(8,128)S(1)} fusion(f32[32,2048]{1,0:T(8,128)} %reshape_squeeze.3, f32[2048,128]{1,0:T(8,128)S(1)} %get-tuple-element.32, f32[2048,128]{1,0:T(8,128)} %get-tuple-element.33), kind=kOutput, calls=%fused_computation.32 | convolution fusion | flops 201850880 | bytes 2392064 | tf_op jit(solution)/shard_map/dot_general | solution.py:160
  21.9 5.6 %all_gather.3 = f32[8,16,2,128]{3,0,2,1:T(8,128)S(1)} all-gather(f32[8,4,2,128]{3,0,2,1:T(8,128)S(1)} %copy.47), channel_id=1, replica_groups=mesh['row_0'=16,'row_1'=4,'row_2'=2,'gz'=4] {'gz'}, dimensions={1}, use_global_device_ids=true | all-gather | bytes 163840 | tf_op jit(solution)/shard_map/all_gather | solution.py:167
  29.3 18.6 %all-to-all-start = ((bf16[8,4,2,128]{0,1,2,3:T(4,128)(2,1)}), bf16[8,4,2,128]{0,1,2,3:T(4,128)(2,1)S(1)}, u32[]{:S(2)}, u32[]{:S(2)}) async-start(bf16[8,4,2,128]{0,1,2,3:T(4,128)(2,1)} %copy.49), calls=%async_computation | async-start | bytes 524288 | tf_op jit(solution)/shard_map/all_to_all | solution.py:174
  49.4 2.2 %fusion.54 = (f32[4,8,4,2048]{3,2,1,0:T(4,128)S(1)}, f32[4,8,4,2048]{3,2,1,0:T(4,128)}) fusion(f32[4,8,4,2048]{3,2,1,0:T(4,128)S(1)} %copy-done.1, f32[4,8,4,1]{3,2,1,0:T(4,128)S(1)} %get-tuple-element.21, f32[4,8,4,2047]{3,2,1,0:T(4,128)S(1)} %get-tuple-element.23, f32[4,8,4,2047]{3,2,1,0:T(4,128)S(1)} %get-tuple-element.22, ...), kind=kLoop, calls=%fused_computation.118 | loop fusion | flops 3670016 | bytes 5242880 | tf_op jit(solution)/shard_map/sub | solution.py:108
  51.7 1.6 %slice.206 = f32[4,8,4,2047]{3,2,1,0:T(4,128)} slice(f32[4,8,4,2048]{3,2,1,0:T(4,128)S(1)} %get-tuple-element.4), slice={[0:4], [0:8], [0:4], [1:2048]} | slice | bytes 2096128 | tf_op jit(solution)/shard_map/jit(_roll_static)/slice | solution.py:108
  53.3 1.7 %multiply_bitcast_fusion.1 = (f32[8,4,2048]{2,1,0:T(4,128)S(1)}, f32[1,8,4,2048]{3,2,1,0:T(4,128)S(1)}, f32[8,4,2048]{2,1,0:T(4,128)S(1)}, f32[8,4,2048]{2,1,0:T(4,128)S(1)}, f32[8,4,2048]{2,1,0:T(4,128)S(1)}) fusion(f32[4,8,4,2048]{3,2,1,0:T(4,128)} %get-tuple-element.5, f32[4,8,4,1]{3,2,1,0:T(4,128)S(1)} %slice.207, f32[4,8,4,2047]{3,2,1,0:T(4,128)} %slice.206), kind=kLoop, calls=%fused_computation.84 | loop fusion | flops 655360 | bytes 2883584 | tf_op jit(solution)/shard_map/mul | solution.py:91
  55.2 1.9 %multiply_subtract_fusion = f32[4,8,4,2048]{3,2,1,0:T(4,128)} fusion(f32[4,8,4,2048]{3,2,1,0:T(4,128)S(1)} %copy-done.5, f32[4,8,4,1]{3,2,1,0:T(4,128)S(1)} %slice.207, f32[4,8,4,2047]{3,2,1,0:T(4,128)S(1)} %copy-done.3, f32[8,4,2048]{2,1,0:T(4,128)S(1)} %get-tuple-element.2, f32[8,4,2048]{2,1,0:T(4,128)S(1)} %get-tuple-element.13, ...), kind=kLoop, calls=%fused_computation.53 | loop fusion | flops 3145728 | bytes 4456464 | tf_op jit(solution)/shard_map/sub | solution.py:91
  57.1 16.0 %all-to-all-done = bf16[8,4,2,128]{0,1,2,3:T(4,128)(2,1)S(1)} async-done(((bf16[8,4,2,128]{0,1,2,3:T(4,128)(2,1)}), bf16[8,4,2,128]{0,1,2,3:T(4,128)(2,1)S(1)}, u32[]{:S(2)}, u32[]{:S(2)}) %all-to-all-start) | async-done | bytes 16416 | tf_op jit(solution)/shard_map/all_to_all | solution.py:174
  73.8 1.2 reshape.121
  75.7 1.6 %reshape.122 = f32[16,4,2,8,4,2,1]{3,2,1,0,4,5,6:T(2,128)} reshape(f32[1024,4,2,1]{0,1,2,3:T(4,128)S(1)} %fusion.12) | data formatting | bytes 65536 | tf_op jit(solution)/shard_map/reshape;reshape | solution.py:50
  77.4 1.9 %copy.76 = f32[16,4,2,8,4,2,1]{3,2,1,5,4,6,0:T(2,128)} copy(f32[16,4,2,8,4,2,1]{3,2,1,0,4,5,6:T(2,128)} %reshape.122) | data formatting | bytes 65536 | tf_op jit(solution)/shard_map/reshape;reshape | solution.py:50
  79.3 2.4 %reshape.123 = f32[16,1,512]{2,1,0:T(1,128)} reshape(f32[16,1,4,2,4,2,8]{6,5,4,3,2,1,0:T(2,128)} %bitcast.102) | data formatting | bytes 65536
  81.7 3.7 %all-to-all-start.1 = ((f32[16,1,512]{2,1,0:T(1,128)}), f32[16,1,512]{2,1,0:T(1,128)S(1)}, u32[]{:S(2)}, u32[]{:S(2)}) async-start(f32[16,1,512]{2,1,0:T(1,128)} %reshape.123), calls=%async_computation.1 | async-start | bytes 65536 | tf_op jit(solution)/shard_map/all_to_all | solution.py:52
  85.5 11.5 %all-to-all-done.1 = f32[16,1,512]{2,1,0:T(1,128)S(1)} async-done(((f32[16,1,512]{2,1,0:T(1,128)}), f32[16,1,512]{2,1,0:T(1,128)S(1)}, u32[]{:S(2)}, u32[]{:S(2)}) %all-to-all-start.1) | async-done | bytes 32800 | tf_op jit(solution)/shard_map/all_to_all | solution.py:52
  98.3 1.6 %reshape.124 = f32[16,1,4,2,4,2,8]{6,5,4,3,2,1,0:T(2,128)} reshape(f32[16,512]{1,0:T(8,128)S(1)} %reduce) | data formatting | bytes 65536
  99.9 1.3 copy.54
  102.0 3.4 %all-to-all-start.2 = ((f32[4,1,2048]{2,1,0:T(1,128)}), f32[4,1,2048]{2,1,0:T(1,128)S(1)}, u32[]{:S(2)}, u32[]{:S(2)}) async-start(f32[4,1,2048]{2,1,0:T(1,128)} %reshape.125), calls=%async_computation.2 | async-start | bytes 65536 | tf_op jit(solution)/shard_map/all_to_all | solution.py:52
  106.8 3.9 %all-to-all-done.2 = f32[4,1,2048]{2,1,0:T(1,128)S(1)} async-done(((f32[4,1,2048]{2,1,0:T(1,128)}), f32[4,1,2048]{2,1,0:T(1,128)S(1)}, u32[]{:S(2)}, u32[]{:S(2)}) %all-to-all-start.2) | async-done | bytes 32800 | tf_op jit(solution)/shard_map/all_to_all | solution.py:52
  112.3 1.7 %reshape.127 = f32[2,1,4096]{2,1,0:T(1,128)} reshape(f32[2,4,4,2,1,8,16]{6,5,4,3,2,1,0:T(8,128)} %copy_bitcast_fusion.1) | data formatting | bytes 65536
  114.1 3.3 %all-to-all-start.3 = ((f32[2,1,4096]{2,1,0:T(1,128)}), f32[2,1,4096]{2,1,0:T(1,128)S(1)}, u32[]{:S(2)}, u32[]{:S(2)}) async-start(f32[2,1,4096]{2,1,0:T(1,128)} %reshape.127), calls=%async_computation.3 | async-start | bytes 65536 | tf_op jit(solution)/shard_map/all_to_all | solution.py:52
  118.3 4.4 %all-to-all-done.3 = f32[2,1,4096]{2,1,0:T(1,128)S(1)} async-done(((f32[2,1,4096]{2,1,0:T(1,128)}), f32[2,1,4096]{2,1,0:T(1,128)S(1)}, u32[]{:S(2)}, u32[]{:S(2)}) %all-to-all-start.3) | async-done | bytes 32800 | tf_op jit(solution)/shard_map/all_to_all | solution.py:52
  124.7 1.2 copy.57
  125.9 3.5 %fusion.2 = f32[32,2048]{1,0:T(8,128)S(1)} fusion(f32[2048,128]{1,0:T(8,128)} %copy-done.4, f32[2048,128]{1,0:T(8,128)} %get-tuple-element.33, f32[256]{0:T(256)S(1)} %pad_maximum_fusion.12, f32[4,8,2,128]{3,2,1,0:T(2,128)S(1)} %bitcast.109), kind=kOutput, calls=%fused_computation.3 | convolution fusion | flops 202375168 | bytes 2393088 | tf_op jit(solution)/shard_map/dot_general | solution.py:178
  132.8 3.5 %collective-permute-start.2 = (f32[1,4,2048]{2,1,0:T(4,128)}, f32[1,4,2048]{2,1,0:T(4,128)}, u32[]{:S(2)}, u32[]{:S(2)}) collective-permute-start(f32[1,4,2048]{2,1,0:T(4,128)} %get-tuple-element.26), channel_id=1, source_target_pairs={{4,0},{8,4},{12,8},{16,12},{20,16},{24,20},{28,24},{32,28},{36,32}... | collective-permute-start | bytes 98312 | tf_op jit(solution)/shard_map/ppermute | solution.py:29
  136.3 3.8 %collective-permute-start.3 = (f32[1,4,2048]{2,1,0:T(4,128)S(1)}, f32[1,4,2048]{2,1,0:T(4,128)}, u32[]{:S(2)}, u32[]{:S(2)}) collective-permute-start(f32[1,4,2048]{2,1,0:T(4,128)S(1)} %get-tuple-element.27), channel_id=1, source_target_pairs={{0,4},{4,8},{8,12},{12,16},{16,20},{20,24},{24,28},{28,32},{32,36}... | collective-permute-start | bytes 98312 | tf_op jit(solution)/shard_map/ppermute | solution.py:27
  140.6 1.3 fusion.39
  142.0 4.8 %collective-permute-done.3 = f32[1,4,2048]{2,1,0:T(4,128)} collective-permute-done((f32[1,4,2048]{2,1,0:T(4,128)S(1)}, f32[1,4,2048]{2,1,0:T(4,128)}, u32[]{:S(2)}, u32[]{:S(2)}) %collective-permute-start.3) | collective-permute-done | bytes 32800 | tf_op jit(solution)/shard_map/ppermute | solution.py:27
  153.8 2.1 %multiply_add_fusion = f32[4,8,4,2048]{3,2,1,0:T(4,128)} fusion(f32[4,8,4,2048]{3,2,1,0:T(4,128)S(1)} %copy-done.1, f32[1,8,4,2048]{3,2,1,0:T(4,128)S(1)} %broadcast.100, f32[1,8,4,2048]{3,2,1,0:T(4,128)S(1)} %fusion.39, f32[1,8,4,2048]{3,2,1,0:T(4,128)S(1)} %fusion.40, f32[4,8,4,2048]{3,2,1,0:T(4,128)S(1)} %copy-done.2, f32[4,8,4,2047]{3,2,1,0:T(4,128)S(1)} %bitcast.101, ...), kind=kLoop, calls=%fused_computation.48 | loop fusion | flops 3670016 | bytes 7077920 | tf_op jit(solution)/shard_map/add | solution.py:132
  (71 shorter events, 24.1 us)
Async XLA Ops:
  0.6 74.5 %copy-start = (bf16[1,1024,1024]{2,1,0:T(8,128)(2,1)S(1)}, bf16[1,1024,1024]{2,1,0:T(8,128)(2,1)}, u32[]{:S(2)}) copy-start(bf16[1,1024,1024]{2,1,0:T(8,128)(2,1)} %param.4) | copy-start | bytes 6291460
  2.7 145.2 %collective-permute-start = (f32[4,2,4,2048]{3,2,1,0:T(4,128)}, f32[4,2,4,2048]{3,2,1,0:T(4,128)}, u32[]{:S(2)}, u32[]{:S(2)}) collective-permute-start(f32[4,2,4,2048]{3,2,1,0:T(4,128)} %get-tuple-element.18), channel_id=1, source_target_pairs={{0,4},{4,8},{8,12},{12,16},{16,20},{20,24},{24,28},{28,32},{32,36}... | collective-permute-start | bytes 786440 | tf_op jit(solution)/shard_map/ppermute | solution.py:27
  7.8 141.1 %collective-permute-start.1 = (f32[4,2,4,2048]{3,2,1,0:T(4,128)}, f32[4,2,4,2048]{3,2,1,0:T(4,128)}, u32[]{:S(2)}, u32[]{:S(2)}) collective-permute-start(f32[4,2,4,2048]{3,2,1,0:T(4,128)} %get-tuple-element.19), channel_id=1, source_target_pairs={{4,0},{8,4},{12,8},{16,12},{20,16},{24,20},{28,24},{32,28},{36,32}... | collective-permute-start | bytes 786440 | tf_op jit(solution)/shard_map/ppermute | solution.py:29
  13.1 5.3 %slice-start = ((f32[4,8,4,2048]{3,2,1,0:T(4,128)}), f32[1,8,4,2048]{3,2,1,0:T(4,128)S(1)}, s32[]{:S(2)}) async-start(f32[4,8,4,2048]{3,2,1,0:T(4,128)} %param.3), calls=%async_computation.4 | async-start | bytes 524288 | tf_op jit(solution)/shard_map/slice | solution.py:122
  18.4 1.0 copy-start.4
  21.9 26.1 %copy-start.1 = (f32[4,8,4,2048]{3,2,1,0:T(4,128)S(1)}, f32[4,8,4,2048]{3,2,1,0:T(4,128)}, u32[]{:S(2)}) copy-start(f32[4,8,4,2048]{3,2,1,0:T(4,128)} %param.3) | copy-start | bytes 3145732
  29.3 43.8 %all-to-all-start = ((bf16[8,4,2,128]{0,1,2,3:T(4,128)(2,1)}), bf16[8,4,2,128]{0,1,2,3:T(4,128)(2,1)S(1)}, u32[]{:S(2)}, u32[]{:S(2)}) async-start(bf16[8,4,2,128]{0,1,2,3:T(4,128)(2,1)} %copy.49), calls=%async_computation | async-start | bytes 524288 | tf_op jit(solution)/shard_map/all_to_all | solution.py:174
  53.3 1.7 %copy-start.3 = (f32[4,8,4,2047]{3,2,1,0:T(4,128)S(1)}, f32[4,8,4,2047]{3,2,1,0:T(4,128)}, u32[]{:S(2)}) copy-start(f32[4,8,4,2047]{3,2,1,0:T(4,128)} %slice.206) | copy-start | bytes 3144196
  53.3 1.9 %copy-start.5 = (f32[4,8,4,2048]{3,2,1,0:T(4,128)S(1)}, f32[4,8,4,2048]{3,2,1,0:T(4,128)}, u32[]{:S(2)}) copy-start(f32[4,8,4,2048]{3,2,1,0:T(4,128)} %get-tuple-element.5) | copy-start | bytes 3145732
  81.7 15.2 %all-to-all-start.1 = ((f32[16,1,512]{2,1,0:T(1,128)}), f32[16,1,512]{2,1,0:T(1,128)S(1)}, u32[]{:S(2)}, u32[]{:S(2)}) async-start(f32[16,1,512]{2,1,0:T(1,128)} %reshape.123), calls=%async_computation.1 | async-start | bytes 65536 | tf_op jit(solution)/shard_map/all_to_all | solution.py:52
  102.0 8.8 %all-to-all-start.2 = ((f32[4,1,2048]{2,1,0:T(1,128)}), f32[4,1,2048]{2,1,0:T(1,128)S(1)}, u32[]{:S(2)}, u32[]{:S(2)}) async-start(f32[4,1,2048]{2,1,0:T(1,128)} %reshape.125), calls=%async_computation.2 | async-start | bytes 65536 | tf_op jit(solution)/shard_map/all_to_all | solution.py:52
  114.1 8.7 %all-to-all-start.3 = ((f32[2,1,4096]{2,1,0:T(1,128)}), f32[2,1,4096]{2,1,0:T(1,128)S(1)}, u32[]{:S(2)}, u32[]{:S(2)}) async-start(f32[2,1,4096]{2,1,0:T(1,128)} %reshape.127), calls=%async_computation.3 | async-start | bytes 65536 | tf_op jit(solution)/shard_map/all_to_all | solution.py:52
  129.4 0.7 copy-start.7
  131.8 15.9 %copy-start.6 = (f32[8,4,2048]{2,1,0:T(4,128)}, f32[8,4,2048]{2,1,0:T(4,128)S(1)}, u32[]{:S(2)}) copy-start(f32[8,4,2048]{2,1,0:T(4,128)S(1)} %reshape.118) | copy-start | bytes 786436
  132.8 9.1 %collective-permute-start.2 = (f32[1,4,2048]{2,1,0:T(4,128)}, f32[1,4,2048]{2,1,0:T(4,128)}, u32[]{:S(2)}, u32[]{:S(2)}) collective-permute-start(f32[1,4,2048]{2,1,0:T(4,128)} %get-tuple-element.26), channel_id=1, source_target_pairs={{4,0},{8,4},{12,8},{16,12},{20,16},{24,20},{28,24},{32,28},{36,32}... | collective-permute-start | bytes 98312 | tf_op jit(solution)/shard_map/ppermute | solution.py:29
  136.3 10.4 %collective-permute-start.3 = (f32[1,4,2048]{2,1,0:T(4,128)S(1)}, f32[1,4,2048]{2,1,0:T(4,128)}, u32[]{:S(2)}, u32[]{:S(2)}) collective-permute-start(f32[1,4,2048]{2,1,0:T(4,128)S(1)} %get-tuple-element.27), channel_id=1, source_target_pairs={{0,4},{4,8},{8,12},{12,16},{16,20},{20,24},{24,28},{28,32},{32,36}... | collective-permute-start | bytes 98312 | tf_op jit(solution)/shard_map/ppermute | solution.py:27
  140.6 7.3 %copy-start.9 = (f32[4,4,2048]{2,1,0:T(4,128)S(1)}, f32[4,4,2048]{2,1,0:T(4,128)}, u32[]{:S(2)}) copy-start(f32[4,4,2048]{2,1,0:T(4,128)} %get-tuple-element.16) | copy-start | bytes 393220
  141.9 7.0 %copy-start.8 = (f32[4,4,2048]{2,1,0:T(4,128)S(1)}, f32[4,4,2048]{2,1,0:T(4,128)}, u32[]{:S(2)}) copy-start(f32[4,4,2048]{2,1,0:T(4,128)} %get-tuple-element.17) | copy-start | bytes 393220
  152.6 1.2 copy-start.2
where the time goes:
time: 157 us; the launch traced here: 156 us
  starting transfers between devices  46.7 us (30%)
  waiting for transfers between devices  40.6 us (26%)
  local copies, waits for them, and re-layouts  29.9 us (19%)
  other arithmetic  23.8 us (15%)
  matrix products  7.55 us (5%)
  blocking collectives  5.56 us (4%)
  between operations  1.7 us (1%)
    all_to_all x3, waiting for transfers between devices, moved_by_axis(): result = lax.all_to_all(result, axes[k], k, k, tiled=True)  19.8 us
    all_to_all x1, starting transfers between devices, body(): lax.all_to_all(mixed_b, ROW, split_axis=3, concat_axis=0, tiled=True)  18.6 us
    all_to_all x1, waiting for transfers between devices, body(): lax.all_to_all(mixed_b, ROW, split_axis=3, concat_axis=0, tiled=True)  16 us
    all_to_all x3, starting transfers between devices, moved_by_axis(): result = lax.all_to_all(result, axes[k], k, k, tiled=True)  10.4 us
    ppermute x2, starting transfers between devices, padded_2(): lax.ppermute(tail, axis, [(i, (i + 1) % count) for i in range(ends)])  8.91 us
    ppermute x2, starting transfers between devices, padded_2(): lax.ppermute(head, axis, [((i + 1) % count, i) for i in range(ends)])  8.77 us
    unnamed x27, local copies, waits for them, and re-layouts  8.61 us
    all_gather x1, blocking collectives, body(): column_all = lax.all_gather(spectrum, 'gz', axis=1, tiled=True)  5.56 us
  transfers between devices with their start and end apart: 8, of which 5 were waited for; matrix products, arithmetic and copies ran while one was open for 33% of the time, Pallas kernels for 0%

commit v1 on v0

v1 whole, which is shorter than its diff:
```python
import functools
import math

import jax
import jax.numpy as jnp
import ml_dtypes
import numpy as np
from jax import lax
from jax.experimental import pallas as pl
from jax.experimental.pallas import tpu as pltpu
from jax.sharding import PartitionSpec as P

NR, NPHI, MODES, ZW = 1024, 2048, 128, 16
ROWS, GZ = 128, 4
DR = 4.0 / NR
DPHI = 2.0 * math.pi / NPHI
DT = 0.2 * min(DR, DPHI)
F32, BF16 = jnp.float32, jnp.bfloat16
MESH = pl.DeviceIdType.MESH
CHUNK = 256


def tables():
    index = np.arange(NPHI)[:, None] * np.arange(MODES)[None, :] % NPHI
    angles = 2.0 * np.pi * index / NPHI
    forward = np.concatenate([np.cos(angles), -np.sin(angles)], axis=1)
    weights = np.where(np.arange(MODES) == 0, 1.0, 2.0) / NPHI
    inverse = forward.T * np.concatenate([weights, weights])[:, None]
    out = []
    for table in (forward, inverse):
        high = table.astype(np.float32).astype(ml_dtypes.bfloat16)
        low = (table - high.astype(np.float64)).astype(np.float32).astype(ml_dtypes.bfloat16)
        out += [high, low]
    return out


def split(x):
    high = x.astype(BF16)
    return high, (x - high.astype(F32)).astype(BF16)


def dot(a, b):
    return jnp.dot(a, b, preferred_element_type=F32)


def iota(shape, dim):
    return lax.broadcasted_iota(jnp.int32, shape, dim)


def minmod_half(a, b):
    return jnp.where(a * b > 0, jnp.where(jnp.abs(a) < jnp.abs(b), a, b), 0.0) * 0.5


def rusanov(left, right, normal):
    v_left = left[normal] / left[0]
    v_right = right[normal] / right[0]
    reach = jnp.maximum(jnp.abs(v_left), jnp.abs(v_right)) + 1.0
    fluxes = []
    for k in range(4):
        both = left[k] * v_left + right[k] * v_right
        if k == normal:
            both = both + (left[0] + right[0])
        fluxes.append(0.5 * (both - reach * (right[k] - left[k])))
    return fluxes


def lanes(column, width):
    return jnp.concatenate([column] * (width // 128), axis=1)


def pair_row(shape):
    return (iota(shape, 0) >= 4).astype(jnp.int32)


def peer(row, k):
    step, low = k // 8, 7 - lax.rem(k, 8)
    half = (step + 1) // 2
    shift = jnp.where(lax.rem(step, 2) == 0, 8 + half, 8 - half)
    z, q = row // 8, lax.rem(row, 8)
    return lax.rem(z + shift, 16) * 8 + (q ^ low)


def exchange_kernel(
    state, green, vertical, t_high, t_low, part, spec,
    S, O, TH, TL, G, SA, msg, X, back, Y, LB, RB, FB, FR, acc,
    sem_in, sem_gs, sem_gr, sem_as, sem_ar, sem_bs, sem_br, sem_hs, sem_hr, sem_out,
):
    row, gz = lax.axis_index("row"), lax.axis_index("gz")

    def load_rows(fields, target, shift, sem):
        for r in range(8):
            t = r + 2 - shift
            pltpu.make_async_copy(
                state.at[fields, r], target.at[fields, t // 2, pl.ds(4 * (t % 2), 4)], sem
            ).start()

    load_rows(pl.ds(0, 1), S, 0, sem_in.at[0])
    load_t = [
        pltpu.make_async_copy(t_high, TH, sem_in.at[1]),
        pltpu.make_async_copy(t_low, TL, sem_in.at[2]),
    ]
    for copy in load_t:
        copy.start()
    load_rows(pl.ds(1, 3), S, 0, sem_in.at[3])
    load_rows(pl.ds(0, 4), O, 1, sem_in.at[4])
    load_g = pltpu.make_async_copy(green, G, sem_in.at[5])
    load_g.start()

    barrier = pltpu.get_barrier_semaphore()

    def greet(k, carry):
        pl.semaphore_signal(barrier, inc=1, device_id=(peer(row, k), gz), device_id_type=MESH)
        return carry

    lax.fori_loop(0, ROWS - 1, greet, 0)
    for k in range(1, GZ):
        pl.semaphore_signal(barrier, inc=1, device_id=(row, gz ^ k), device_id_type=MESH)

    pltpu.make_async_copy(S.at[0, pl.ds(1, 4)], S.at[0, pl.ds(1, 4)], sem_in.at[0]).wait()
    density = S[0, pl.ds(1, 4)].reshape(32, NPHI)
    high, low = split(density)
    load_t[0].wait()
    stacked = dot(jnp.concatenate([high, low], axis=0), TH[...])
    load_t[1].wait()
    own = pl.ds(pl.multiple_of(gz * 32, 32), 32)
    SA[own, :] = stacked[:32] + stacked[32:] + dot(high, TL[...])

    pl.semaphore_wait(barrier, ROWS - 1 + GZ - 1)
    gathers = []
    for k in range(1, GZ):
        gathers.append(
            pltpu.make_async_remote_copy(
                SA.at[own], SA.at[own], sem_gs.at[k], sem_gr.at[k],
                device_id=(row, gz ^ k), device_id_type=MESH,
            )
        )
        gathers[-1].start()

    a_row, a_col = iota((256, 16), 0), iota((256, 16), 1)
    pick_y = (a_col == 4 * ((a_row >> 5) & 3) + (a_row & 3)).astype(BF16)
    b_row, b_col = iota((16, 128), 0), iota((16, 128), 1)
    pick_z = (b_row == 4 * gz + (b_col & 3)).astype(BF16)
    w_row, w_col = iota((256, 128), 0), iota((256, 128), 1)
    w_keep = ((w_row >> 7) == (w_col >> 6)) & (((w_row >> 2) & 7) == ((w_col >> 2) & 15))
    weights = []
    for piece in split(vertical[...]):
        rows_y = lax.dot_general(
            pick_y, piece, (((1,), (1,)), ((), ())), preferred_element_type=F32
        ).astype(BF16)
        weights.append(jnp.where(w_keep, dot(rows_y, pick_z), 0.0).astype(BF16))
    for copy in gathers:
        copy.wait()
    turned = jnp.concatenate([SA[:, :MODES].T, SA[:, MODES:].T], axis=1)
    high, low = split(turned)
    mixed = dot(high, weights[0]) + dot(low, weights[0]) + dot(high, weights[1])
    msg[...] = mixed.astype(BF16).astype(F32)

    def send_forward(k, carry):
        d = peer(row, k)
        pltpu.make_async_remote_copy(
            msg.at[pl.ds(d, 1)], X.at[row], sem_as, sem_ar, device_id=(d, gz), device_id_type=MESH
        ).start()
        return carry

    lax.fori_loop(0, ROWS - 1, send_forward, 0)
    X[row] = msg[pl.ds(row, 1), :]

    pltpu.make_async_copy(
        S.at[pl.ds(1, 3), pl.ds(1, 4)], S.at[pl.ds(1, 3), pl.ds(1, 4)], sem_in.at[3]
    ).wait()
    pltpu.make_async_copy(O.at[:, pl.ds(0, 4)], O.at[:, pl.ds(0, 4)], sem_in.at[4]).wait()
    down = pltpu.make_async_remote_copy(
        S.at[:, 1], S.at[:, 5], sem_hs.at[0], sem_hr.at[0],
        device_id=(jnp.maximum(row - 1, 0), gz), device_id_type=MESH,
    )
    up = pltpu.make_async_remote_copy(
        S.at[:, 4], S.at[:, 0], sem_hs.at[1], sem_hr.at[1],
        device_id=(jnp.minimum(row + 1, ROWS - 1), gz), device_id_type=MESH,
    )

    @pl.when(row > 0)
    def _():
        down.start()

    @pl.when(row < ROWS - 1)
    def _():
        up.start()

    first = row * 8

    def azimuth(j, carry):
        centre = 1.0 + ((first + 2 * j + pair_row((8, 128))).astype(F32) + 0.5) * DR
        inverse_r = lanes(1.0 / centre, CHUNK)
        for k in range(4):
            u = S[k, j + 1]
            back_diff = u - pltpu.roll(u, 1, 1)
            slope = minmod_half(back_diff, pltpu.roll(back_diff, NPHI - 1, 1))
            LB[k] = u + slope
            RB[k] = pltpu.roll(u - slope, NPHI - 1, 1)

        for c in range(NPHI // CHUNK):
            at = pl.ds(c * CHUNK, CHUNK)
            fluxes = rusanov([LB[k, :, at] for k in range(4)], [RB[k, :, at] for k in range(4)], 2)
            for k in range(4):
                FB[k, :, at] = fluxes[k]

        for k in range(4):
            flux = FB[k]
            LB[k] = flux - pltpu.roll(flux, 1, 1)

        for c in range(NPHI // CHUNK):
            at = pl.ds(c * CHUNK, CHUNK)
            u = [S[k, j + 1, :, at] for k in range(4)]
            spin = u[2] / u[0]
            gain = [None, u[2] * spin + u[0], -(u[1] * spin), None]
            for k in range(4):
                change = LB[k, :, at] * (-1.0 / DPHI)
                if gain[k] is not None:
                    change = change + gain[k]
                acc[k, j, :, at] = u[k] + DT * inverse_r * change
        return carry

    lax.fori_loop(0, 4, azimuth, 0)

    def radial(j, c):
        at = pl.ds(pl.multiple_of(c * CHUNK, CHUNK), CHUNK)
        face = lanes(1.0 + (first + 2 * j + pair_row((8, 128))).astype(F32) * DR, CHUNK)
        left, right = [], []
        for k in range(4):
            a0, a1, a2, a3 = S[k, j, :, at], O[k, j, :, at], S[k, j + 1, :, at], O[k, j + 1, :, at]
            middle = a2 - a1
            left.append(a1 + minmod_half(a1 - a0, middle))
            right.append(a2 - minmod_half(middle, a3 - a2))
        fluxes = rusanov(left, right, 1)
        for k in range(4):
            FR[k, j, :, at] = face * fluxes[k]

    pieces = NPHI // CHUNK

    def inner(i, carry):
        radial(1 + i // pieces, lax.rem(i, pieces))
        return carry

    lax.fori_loop(0, 2 * pieces, inner, 0)

    pltpu.make_async_copy(X.at[pl.ds(0, ROWS - 1)], X.at[pl.ds(0, ROWS - 1)], sem_ar).wait()
    load_g.wait()
    sub, lane = iota((ROWS, 8, 128), 1), iota((ROWS, 8, 128), 2)
    group = (lane >> 2) & 15
    spread = jnp.where(group == sub, jnp.broadcast_to(X[...], (ROWS, 8, 128)), 0.0)
    f_row, f_col = iota((128, 128), 0), iota((128, 128), 1)
    fold = (((f_row >> 6) == (f_col >> 6)) & ((f_row & 3) == (f_col & 3))).astype(BF16)
    columns = dot(spread.reshape(NR, 128).astype(BF16), fold).astype(BF16)
    solved = dot(G[...], columns).reshape(ROWS, 8, 128)
    keep = (group == sub + 1) | ((group == 0) & (sub == 7)) | ((group == 9) & (sub == 0))
    rows = jnp.sum(jnp.where(keep, solved, 0.0), axis=1)
    f_group = (f_col >> 2) & 15
    back[...] = jnp.where(
        f_group == 0, pltpu.roll(rows, 1, 0),
        jnp.where(f_group == 9, pltpu.roll(rows, ROWS - 1, 0), rows),
    )

    def send_back(k, carry):
        d = peer(row, k)
        pltpu.make_async_remote_copy(
            back.at[pl.ds(d, 1)], Y.at[pl.ds(row, 1)], sem_bs, sem_br,
            device_id=(d, gz), device_id_type=MESH,
        ).start()
        return carry

    lax.fori_loop(0, ROWS - 1, send_back, 0)
    Y[pl.ds(row, 1), :] = back[pl.ds(row, 1), :]

    @pl.when(row > 0)
    def _():
        down.wait_send()
        up.wait_recv()

    @pl.when(row < ROWS - 1)
    def _():
        up.wait_send()
        down.wait_recv()

    @pl.when(row == 0)
    def _():
        for k in range(4):
            S[k, 0, pl.ds(0, 4)] = S[k, 1, pl.ds(0, 4)]
            S[k, 0, pl.ds(4, 4)] = S[k, 1, pl.ds(0, 4)]

    @pl.when(row == ROWS - 1)
    def _():
        for k in range(4):
            S[k, 5, pl.ds(0, 4)] = S[k, 4, pl.ds(4, 4)]
            S[k, 5, pl.ds(4, 4)] = S[k, 4, pl.ds(4, 4)]

    for k in range(4):
        O[k, 0, pl.ds(0, 4)] = S[k, 0, pl.ds(4, 4)]
        O[k, 4, pl.ds(4, 4)] = S[k, 5, pl.ds(0, 4)]
        O[k, 5, pl.ds(0, 4)] = S[k, 5, pl.ds(4, 4)]
        O[k, 5, pl.ds(4, 4)] = S[k, 5, pl.ds(4, 4)]

    def edges(i, carry):
        piece = lax.rem(i, pieces)
        which = i // pieces
        radial(jnp.where(which == 0, 0, which + 2), piece)
        return carry

    lax.fori_loop(0, 3 * pieces, edges, 0)

    def gather_radial(i, carry):
        j, c = i // pieces, lax.rem(i, pieces)
        at = pl.ds(pl.multiple_of(c * CHUNK, CHUNK), CHUNK)
        centre = 1.0 + ((first + 2 * j + pair_row((8, 128))).astype(F32) + 0.5) * DR
        scale = lanes((DT / DR) / centre, CHUNK)
        second = iota((8, CHUNK), 0) >= 4
        for k in range(4):
            low_face = FR[k, j, :, at]
            high_face = pltpu.roll(jnp.where(second, low_face, FR[k, j + 1, :, at]), 4, 0)
            acc[k, j, :, at] = acc[k, j, :, at] - scale * (high_face - low_face)
        return carry

    lax.fori_loop(0, 4 * pieces, gather_radial, 0)
    out_part = pltpu.make_async_copy(acc, part, sem_out.at[0])
    out_part.start()

    pltpu.make_async_copy(Y.at[pl.ds(0, ROWS - 1)], Y.at[pl.ds(0, ROWS - 1)], sem_br).wait()
    out_spec = pltpu.make_async_copy(Y, spec, sem_out.at[1])
    out_spec.start()
    pltpu.make_async_copy(X.at[pl.ds(0, ROWS - 1)], X.at[pl.ds(0, ROWS - 1)], sem_as).wait()
    pltpu.make_async_copy(Y.at[pl.ds(0, ROWS - 1)], Y.at[pl.ds(0, ROWS - 1)], sem_bs).wait()
    out_part.wait()
    out_spec.wait()


def finish_kernel(state, part, spec, t_high, t_low, new_state, potential, D, M, TH, TL, PT, OUT, sem):
    row = lax.axis_index("row")
    load_t = [
        pltpu.make_async_copy(t_high, TH, sem.at[0]),
        pltpu.make_async_copy(t_low, TL, sem.at[1]),
    ]
    for copy in load_t:
        copy.start()
    for r in range(8):
        pltpu.make_async_copy(
            state.at[0, r], D.at[r // 2, pl.ds(4 * (r % 2), 4)], sem.at[2]
        ).start()
    load_m = pltpu.make_async_copy(part.at[pl.ds(1, 2)], M, sem.at[3])
    load_m.start()
    plain = []
    for i, k in enumerate((0, 3)):
        for r in range(8):
            plain.append(
                pltpu.make_async_copy(
                    part.at[k, r // 2, pl.ds(4 * (r % 2), 4)], new_state.at[k, r], sem.at[4 + i]
                )
            )
            plain[-1].start()

    turned = spec[...].T
    pieces = []
    for c in range(2):
        base = 64 * c
        own = turned[base + 4 : base + 36]
        ext = turned[base : base + 40]
        before = jnp.where(row == 0, turned[base + 4 : base + 8], turned[base : base + 4])
        after = jnp.where(row == ROWS - 1, turned[base + 32 : base + 36], turned[base + 36 : base + 40])
        pieces.append(jnp.concatenate([own, before, ext[4:36], after], axis=0))
    high, low = split(jnp.concatenate(pieces, axis=1))
    load_t[0].wait()
    total = dot(jnp.concatenate([high, low], axis=0), TH[...])
    load_t[1].wait()
    PT[...] = total[:72] + total[72:] + dot(high, TL[...])

    for r in range(8):
        pltpu.make_async_copy(PT.at[pl.ds(4 * r, 4)], potential.at[r], sem.at[6]).start()
    pltpu.make_async_copy(D, D, sem.at[2]).wait()
    load_m.wait()
    for j in range(4):
        centre = 1.0 + ((row * 8 + 2 * j + pair_row((8, 128))).astype(F32) + 0.5) * DR
        scale = lanes((DT / (2.0 * DPHI)) / centre, NPHI)
        mine = PT[pl.ds(8 * j, 8)]
        slope = PT[pl.ds(40 + 8 * j, 8)] - PT[pl.ds(32 + 8 * j, 8)]
        around = pltpu.roll(mine, NPHI - 1, 1) - pltpu.roll(mine, 1, 1)
        OUT[0, j] = M[0, j] - (DT / (2.0 * DR)) * D[j] * slope
        OUT[1, j] = M[1, j] - scale * D[j] * around
        for i in range(2):
            for h in range(2):
                pltpu.make_async_copy(
                    OUT.at[i, j, pl.ds(4 * h, 4)], new_state.at[1 + i, 2 * j + h], sem.at[7]
                ).start()
    pltpu.make_async_copy(OUT, OUT, sem.at[7]).wait()
    pltpu.make_async_copy(PT.at[pl.ds(0, 32)], PT.at[pl.ds(0, 32)], sem.at[6]).wait()
    for i in range(2):
        pltpu.make_async_copy(M.at[0], M.at[0], sem.at[4 + i]).wait()


def body(state, green, vertical):
    f_high, f_low, i_high, i_low = (jnp.asarray(t) for t in tables())
    anywhere = pl.BlockSpec(memory_space=pl.ANY)
    vmem = pl.BlockSpec(memory_space=pltpu.VMEM)
    dma = pltpu.SemaphoreType.DMA
    pair = (8, NPHI)
    part, spec = pl.pallas_call(
        exchange_kernel,
        out_shape=(
            jax.ShapeDtypeStruct((4, 4, *pair), F32),
            jax.ShapeDtypeStruct((ROWS, 128), F32),
        ),
        in_specs=[anywhere, anywhere, vmem, anywhere, anywhere],
        out_specs=(anywhere, anywhere),
        scratch_shapes=[
            pltpu.VMEM((4, 6, *pair), F32),
            pltpu.VMEM((4, 6, *pair), F32),
            pltpu.VMEM((NPHI, 2 * MODES), BF16),
            pltpu.VMEM((NPHI, 2 * MODES), BF16),
            pltpu.VMEM((NR, NR), BF16),
            pltpu.VMEM((128, 2 * MODES), F32),
            pltpu.VMEM((ROWS, 128), F32),
            pltpu.VMEM((ROWS, 1, 128), F32),
            pltpu.VMEM((ROWS, 128), F32),
            pltpu.VMEM((ROWS, 128), F32),
            pltpu.VMEM((4, *pair), F32),
            pltpu.VMEM((4, *pair), F32),
            pltpu.VMEM((4, *pair), F32),
            pltpu.VMEM((4, 5, *pair), F32),
            pltpu.VMEM((4, 4, *pair), F32),
            dma((6,)), dma((4,)), dma((4,)), dma, dma, dma, dma, dma((2,)), dma((2,)), dma((2,)),
        ],
        compiler_params=pltpu.CompilerParams(
            collective_id=0, has_side_effects=True, vmem_limit_bytes=40 << 20
        ),
        name="exchange",
    )(state, green.reshape(NR, NR), vertical, f_high, f_low)
    return pl.pallas_call(
        finish_kernel,
        out_shape=(
            jax.ShapeDtypeStruct((4, 8, 4, NPHI), F32),
            jax.ShapeDtypeStruct((8, 4, NPHI), F32),
        ),
        in_specs=[anywhere, anywhere, vmem, anywhere, anywhere],
        out_specs=(anywhere, anywhere),
        scratch_shapes=[
            pltpu.VMEM((4, *pair), F32),
            pltpu.VMEM((2, 4, *pair), F32),
            pltpu.VMEM((2 * MODES, NPHI), BF16),
            pltpu.VMEM((2 * MODES, NPHI), BF16),
            pltpu.VMEM((72, NPHI), F32),
            pltpu.VMEM((2, 4, *pair), F32),
            dma((8,)),
        ],
        compiler_params=pltpu.CompilerParams(vmem_limit_bytes=24 << 20),
        name="finish",
    )(state, part, spec, i_high, i_low)


def solution(mesh):
    placed = (P(None, "row", "gz", None), P("row", None, None), P())
    return jax.shard_map(
        body,
        mesh=mesh,
        in_specs=placed,
        out_specs=(P(None, "row", "gz", None), P("row", "gz", None)),
        check_vma=False,
    )
```

time: 157 us -> 53.9 us (0.34)
  the two profiles are of different devices: /device:TPU:32 before, /device:TPU:6 now
where the time goes in v1:
time: 53.9 us; the launch traced here: 53.6 us
  Pallas kernels  47 us (87%)
  local copies, waits for them, and re-layouts  5.96 us (11%)
  between operations  0.67 us (1%)
    pallas_call x1, Pallas kernels, body(): pl.pallas_call(exchange_kernel, out_shape=(jax.ShapeDtypeStruct((4, 4, *p...  45 us
    unnamed x14, local copies, waits for them, and re-layouts  5.96 us
    pallas_call x1, Pallas kernels, body(): pl.pallas_call(finish_kernel, out_shape=(jax.ShapeDtypeStruct((4, 8, 4, N...  1.94 us

profile of v1, /device:TPU:6, one launch (start us, length us, event | category | flops | bytes accessed | tf_op | source)
XLA Modules:
  0.0 53.6 jit_solution(7401602546561962645)
XLA Ops:
  0.6 0.0 copy-start
  0.6 1.2 %copy-done = f32[4,8,4,2048]{3,2,1,0:T(4,128)S(1)} copy-done((f32[4,8,4,2048]{3,2,1,0:T(4,128)S(1)}, f32[4,8,4,2048]{3,2,1,0:T(4,128)}, u32[]{:S(2)}) %copy-start) | copy-done | bytes 1048600
  1.9 0.0 copy-start.1
  1.9 1.6 %copy-done.1 = bf16[1,1024,1024]{2,1,0:T(8,128)(2,1)S(1)} copy-done((bf16[1,1024,1024]{2,1,0:T(8,128)(2,1)S(1)}, bf16[1,1024,1024]{2,1,0:T(8,128)(2,1)}, u32[]{:S(2)}) %copy-start.1) | copy-done | bytes 2097176
  3.4 0.0 copy-start.2
  3.4 1.2 %copy-done.2 = bf16[2048,256]{1,0:T(8,128)(2,1)S(1)} copy-done((bf16[2048,256]{1,0:T(8,128)(2,1)S(1)}, bf16[2048,256]{1,0:T(8,128)(2,1)}, u32[]{:S(2)}) %copy-start.2) | copy-done | bytes 1048600
  4.7 0.0 copy-start.3
  4.7 1.2 %copy-done.3 = bf16[2048,256]{1,0:T(8,128)(2,1)S(1)} copy-done((bf16[2048,256]{1,0:T(8,128)(2,1)S(1)}, bf16[2048,256]{1,0:T(8,128)(2,1)}, u32[]{:S(2)}) %copy-start.3) | copy-done | bytes 1048600
  5.9 0.0 copy-start.6
  5.9 0.7 %copy-done.6 = f32[16,16]{1,0:T(8,128)S(1)} copy-done((f32[16,16]{1,0:T(8,128)S(1)}, f32[16,16]{1,0:T(8,128)}, u32[]{:S(2)}) %copy-start.6) | copy-done | bytes 1048
  6.6 0.0 copy-start.4
  6.6 0.0 copy-start.5
  6.6 45.0 %exchange.1 = (f32[4,4,8,2048]{3,2,1,0:T(8,128)S(1)}, f32[128,128]{1,0:T(8,128)S(1)}) custom-call(f32[4,8,4,2048]{3,2,1,0:T(4,128)S(1)} %copy-done, bf16[1024,1024]{1,0:T(8,128)(2,1)S(1)} %bitcast.1, f32[16,16]{1,0:T(8,128)S(1)} %copy-done.6, bf16[2048,256]{1,0:T(8,128)(2,1)S(1)} %copy-done.3, bf16[2048,256]{1,0:T(8,128)(2,1)S(1)} %copy-done.2), custom_call_target="tpu_custom_call" | custom-call | tf_op jit(solution)/shard_map/exchange/pallas_call | solution.py:403
  51.6 0.0 copy-done.4
  51.7 0.0 copy-done.5
  51.7 1.9 %finish.1 = (f32[4,8,4,2048]{3,2,1,0:T(4,128)}, f32[8,4,2048]{2,1,0:T(4,128)}) custom-call(f32[4,8,4,2048]{3,2,1,0:T(4,128)S(1)} %copy-done, f32[4,4,8,2048]{3,2,1,0:T(8,128)S(1)} %get-tuple-element.4.part, f32[128,128]{1,0:T(8,128)S(1)} %get-tuple-element.5.spec, bf16[256,2048]{1,0:T(8,128)(2,1)S(1)} %copy-done.5, bf16[256,2048]{1,0:T(8,128)(2,1)S(1)} %copy-done.4), custom_call_target="tpu_custom_call" | custom-call | tf_op jit(solution)/shard_map/finish/pallas_call | solution.py:434
Async XLA Ops:
  0.6 1.2 %copy-start = (f32[4,8,4,2048]{3,2,1,0:T(4,128)S(1)}, f32[4,8,4,2048]{3,2,1,0:T(4,128)}, u32[]{:S(2)}) copy-start(f32[4,8,4,2048]{3,2,1,0:T(4,128)} %state.3) | copy-start | bytes 3145732
  1.9 1.6 %copy-start.1 = (bf16[1,1024,1024]{2,1,0:T(8,128)(2,1)S(1)}, bf16[1,1024,1024]{2,1,0:T(8,128)(2,1)}, u32[]{:S(2)}) copy-start(bf16[1,1024,1024]{2,1,0:T(8,128)(2,1)} %param.8) | copy-start | bytes 6291460
  3.4 1.2 %copy-start.2 = (bf16[2048,256]{1,0:T(8,128)(2,1)S(1)}, bf16[2048,256]{1,0:T(8,128)(2,1)}, u32[]{:S(2)}) copy-start(bf16[2048,256]{1,0:T(8,128)(2,1)} %constant.9.clone.t_low) | copy-start | bytes 3145732
  4.7 1.2 %copy-start.3 = (bf16[2048,256]{1,0:T(8,128)(2,1)S(1)}, bf16[2048,256]{1,0:T(8,128)(2,1)}, u32[]{:S(2)}) copy-start(bf16[2048,256]{1,0:T(8,128)(2,1)} %constant.8.clone.t_high) | copy-start | bytes 3145732
  5.9 0.7 %copy-start.6 = (f32[16,16]{1,0:T(8,128)S(1)}, f32[16,16]{1,0:T(8,128)}, u32[]{:S(2)}) copy-start(f32[16,16]{1,0:T(8,128)} %vertical.1) | copy-start | bytes 3076
  6.6 45.1 %copy-start.4 = (bf16[256,2048]{1,0:T(8,128)(2,1)S(1)}, bf16[256,2048]{1,0:T(8,128)(2,1)}, u32[]{:S(2)}) copy-start(bf16[256,2048]{1,0:T(8,128)(2,1)} %constant.11.clone.t_low) | copy-start | bytes 3145732
  6.6 45.1 %copy-start.5 = (bf16[256,2048]{1,0:T(8,128)(2,1)S(1)}, bf16[256,2048]{1,0:T(8,128)(2,1)}, u32[]{:S(2)}) copy-start(bf16[256,2048]{1,0:T(8,128)(2,1)} %constant.10.clone.t_high) | copy-start | bytes 3145732

commit v2 on v1

--- a/solution.py
+++ b/solution.py
@@ -82,7 +82,7 @@
 
 def exchange_kernel(
     state, green, vertical, t_high, t_low, part, spec,
-    S, O, TH, TL, G, SA, msg, X, back, Y, LB, RB, FB, FR, acc,
+    V, HO, HI, S, O, TH, TL, G, SA, msg, X, back, Y, LB, RB, FB, FR, acc,
     sem_in, sem_gs, sem_gr, sem_as, sem_ar, sem_bs, sem_br, sem_hs, sem_hr, sem_out,
 ):
     row, gz = lax.axis_index("row"), lax.axis_index("gz")
@@ -105,6 +105,8 @@
     load_rows(pl.ds(0, 4), O, 1, sem_in.at[4])
     load_g = pltpu.make_async_copy(green, G, sem_in.at[5])
     load_g.start()
+    load_v = pltpu.make_async_copy(vertical, V, sem_in.at[6])
+    load_v.start()
 
     barrier = pltpu.get_barrier_semaphore()
 
@@ -112,9 +114,9 @@
         pl.semaphore_signal(barrier, inc=1, device_id=(peer(row, k), gz), device_id_type=MESH)
         return carry
 
-    lax.fori_loop(0, ROWS - 1, greet, 0)
     for k in range(1, GZ):
         pl.semaphore_signal(barrier, inc=1, device_id=(row, gz ^ k), device_id_type=MESH)
+    lax.fori_loop(0, ROWS - 1, greet, 0)
 
     pltpu.make_async_copy(S.at[0, pl.ds(1, 4)], S.at[0, pl.ds(1, 4)], sem_in.at[0]).wait()
     density = S[0, pl.ds(1, 4)].reshape(32, NPHI)
@@ -143,7 +145,8 @@
     w_row, w_col = iota((256, 128), 0), iota((256, 128), 1)
     w_keep = ((w_row >> 7) == (w_col >> 6)) & (((w_row >> 2) & 7) == ((w_col >> 2) & 15))
     weights = []
-    for piece in split(vertical[...]):
+    load_v.wait()
+    for piece in split(V[...]):
         rows_y = lax.dot_general(
             pick_y, piece, (((1,), (1,)), ((), ())), preferred_element_type=F32
         ).astype(BF16)
@@ -169,12 +172,14 @@
         S.at[pl.ds(1, 3), pl.ds(1, 4)], S.at[pl.ds(1, 3), pl.ds(1, 4)], sem_in.at[3]
     ).wait()
     pltpu.make_async_copy(O.at[:, pl.ds(0, 4)], O.at[:, pl.ds(0, 4)], sem_in.at[4]).wait()
+    for side, j in ((0, 1), (1, 4)):
+        HO[side] = S[:, j].reshape(32, NPHI).astype(BF16)
     down = pltpu.make_async_remote_copy(
-        S.at[:, 1], S.at[:, 5], sem_hs.at[0], sem_hr.at[0],
+        HO.at[0], HI.at[0], sem_hs.at[0], sem_hr.at[0],
         device_id=(jnp.maximum(row - 1, 0), gz), device_id_type=MESH,
     )
     up = pltpu.make_async_remote_copy(
-        S.at[:, 4], S.at[:, 0], sem_hs.at[1], sem_hr.at[1],
+        HO.at[1], HI.at[1], sem_hs.at[1], sem_hr.at[1],
         device_id=(jnp.minimum(row + 1, ROWS - 1), gz), device_id_type=MESH,
     )
 
@@ -212,6 +217,7 @@
             at = pl.ds(c * CHUNK, CHUNK)
             u = [S[k, j + 1, :, at] for k in range(4)]
             spin = u[2] / u[0]
+            acc[4, j, :, at] = DT * u[0]
             gain = [None, u[2] * spin + u[0], -(u[1] * spin), None]
             for k in range(4):
                 change = LB[k, :, at] * (-1.0 / DPHI)
@@ -281,6 +287,14 @@
         up.wait_send()
         down.wait_recv()
 
+    @pl.when(row > 0)
+    def _():
+        S[:, 0] = HI[1].astype(F32).reshape(4, 8, NPHI)
+
+    @pl.when(row < ROWS - 1)
+    def _():
+        S[:, 5] = HI[0].astype(F32).reshape(4, 8, NPHI)
+
     @pl.when(row == 0)
     def _():
         for k in range(4):
@@ -332,18 +346,18 @@
     out_spec.wait()
 
 
-def finish_kernel(state, part, spec, t_high, t_low, new_state, potential, D, M, TH, TL, PT, OUT, sem):
+def finish_kernel(part, spec, t_high, t_low, new_state, potential, Y, D, M, TH, TL, PT, OUT, sem):
     row = lax.axis_index("row")
+    load_y = pltpu.make_async_copy(spec, Y, sem.at[8])
+    load_y.start()
     load_t = [
         pltpu.make_async_copy(t_high, TH, sem.at[0]),
         pltpu.make_async_copy(t_low, TL, sem.at[1]),
     ]
     for copy in load_t:
         copy.start()
-    for r in range(8):
-        pltpu.make_async_copy(
-            state.at[0, r], D.at[r // 2, pl.ds(4 * (r % 2), 4)], sem.at[2]
-        ).start()
+    load_d = pltpu.make_async_copy(part.at[4], D, sem.at[2])
+    load_d.start()
     load_m = pltpu.make_async_copy(part.at[pl.ds(1, 2)], M, sem.at[3])
     load_m.start()
     plain = []
@@ -356,7 +370,8 @@
             )
             plain[-1].start()
 
-    turned = spec[...].T
+    load_y.wait()
+    turned = Y[...].T
     pieces = []
     for c in range(2):
         base = 64 * c
@@ -373,15 +388,15 @@
 
     for r in range(8):
         pltpu.make_async_copy(PT.at[pl.ds(4 * r, 4)], potential.at[r], sem.at[6]).start()
-    pltpu.make_async_copy(D, D, sem.at[2]).wait()
+    load_d.wait()
     load_m.wait()
     for j in range(4):
         centre = 1.0 + ((row * 8 + 2 * j + pair_row((8, 128))).astype(F32) + 0.5) * DR
-        scale = lanes((DT / (2.0 * DPHI)) / centre, NPHI)
+        scale = lanes((1.0 / (2.0 * DPHI)) / centre, NPHI)
         mine = PT[pl.ds(8 * j, 8)]
         slope = PT[pl.ds(40 + 8 * j, 8)] - PT[pl.ds(32 + 8 * j, 8)]
         around = pltpu.roll(mine, NPHI - 1, 1) - pltpu.roll(mine, 1, 1)
-        OUT[0, j] = M[0, j] - (DT / (2.0 * DR)) * D[j] * slope
+        OUT[0, j] = M[0, j] - (1.0 / (2.0 * DR)) * D[j] * slope
         OUT[1, j] = M[1, j] - scale * D[j] * around
         for i in range(2):
             for h in range(2):
@@ -397,18 +412,20 @@
 def body(state, green, vertical):
     f_high, f_low, i_high, i_low = (jnp.asarray(t) for t in tables())
     anywhere = pl.BlockSpec(memory_space=pl.ANY)
-    vmem = pl.BlockSpec(memory_space=pltpu.VMEM)
     dma = pltpu.SemaphoreType.DMA
     pair = (8, NPHI)
     part, spec = pl.pallas_call(
         exchange_kernel,
         out_shape=(
-            jax.ShapeDtypeStruct((4, 4, *pair), F32),
+            jax.ShapeDtypeStruct((5, 4, *pair), F32),
             jax.ShapeDtypeStruct((ROWS, 128), F32),
         ),
-        in_specs=[anywhere, anywhere, vmem, anywhere, anywhere],
+        in_specs=[anywhere] * 5,
         out_specs=(anywhere, anywhere),
         scratch_shapes=[
+            pltpu.VMEM((ZW, ZW), F32),
+            pltpu.VMEM((2, 32, NPHI), BF16),
+            pltpu.VMEM((2, 32, NPHI), BF16),
             pltpu.VMEM((4, 6, *pair), F32),
             pltpu.VMEM((4, 6, *pair), F32),
             pltpu.VMEM((NPHI, 2 * MODES), BF16),
@@ -423,11 +440,11 @@
             pltpu.VMEM((4, *pair), F32),
             pltpu.VMEM((4, *pair), F32),
             pltpu.VMEM((4, 5, *pair), F32),
-            pltpu.VMEM((4, 4, *pair), F32),
-            dma((6,)), dma((4,)), dma((4,)), dma, dma, dma, dma, dma((2,)), dma((2,)), dma((2,)),
+            pltpu.VMEM((5, 4, *pair), F32),
+            dma((7,)), dma((4,)), dma((4,)), dma, dma, dma, dma, dma((2,)), dma((2,)), dma((2,)),
         ],
         compiler_params=pltpu.CompilerParams(
-            collective_id=0, has_side_effects=True, vmem_limit_bytes=40 << 20
+            collective_id=0, has_side_effects=True, vmem_limit_bytes=60 << 20
         ),
         name="exchange",
     )(state, green.reshape(NR, NR), vertical, f_high, f_low)
@@ -437,20 +454,21 @@
             jax.ShapeDtypeStruct((4, 8, 4, NPHI), F32),
             jax.ShapeDtypeStruct((8, 4, NPHI), F32),
         ),
-        in_specs=[anywhere, anywhere, vmem, anywhere, anywhere],
+        in_specs=[anywhere] * 4,
         out_specs=(anywhere, anywhere),
         scratch_shapes=[
+            pltpu.VMEM((ROWS, 128), F32),
             pltpu.VMEM((4, *pair), F32),
             pltpu.VMEM((2, 4, *pair), F32),
             pltpu.VMEM((2 * MODES, NPHI), BF16),
             pltpu.VMEM((2 * MODES, NPHI), BF16),
             pltpu.VMEM((72, NPHI), F32),
             pltpu.VMEM((2, 4, *pair), F32),
-            dma((8,)),
+            dma((9,)),
         ],
-        compiler_params=pltpu.CompilerParams(vmem_limit_bytes=24 << 20),
+        compiler_params=pltpu.CompilerParams(vmem_limit_bytes=60 << 20),
         name="finish",
-    )(state, part, spec, i_high, i_low)
+    )(part, spec, i_high, i_low)
 
 
 def solution(mesh):

time: 53.9 us -> 61 us (1.13)
  the two profiles are of different devices: /device:TPU:6 before, /device:TPU:1 now
where the time goes in v2:
time: 61 us; the launch traced here: 60.5 us
  Pallas kernels  59.9 us (98%)
  between operations  0.64 us (1%)
    pallas_call x1, Pallas kernels, body(): pl.pallas_call(exchange_kernel, out_shape=(jax.ShapeDtypeStruct((5, 4, *p...  42.8 us
    pallas_call x1, Pallas kernels, body(): pl.pallas_call(finish_kernel, out_shape=(jax.ShapeDtypeStruct((4, 8, 4, N...  17.1 us

profile of v2, /device:TPU:1, one launch (start us, length us, event | category | flops | bytes accessed | tf_op | source)
XLA Modules:
  0.0 60.5 jit_solution(12446053125877471508)
XLA Ops:
  0.6 42.8 %exchange.1 = (f32[5,4,8,2048]{3,2,1,0:T(8,128)}, f32[128,128]{1,0:T(8,128)}) custom-call(f32[4,8,4,2048]{3,2,1,0:T(4,128)} %state.1, bf16[1024,1024]{1,0:T(8,128)(2,1)} %bitcast.1, f32[16,16]{1,0:T(8,128)} %vertical.1, bf16[2048,256]{1,0:T(8,128)(2,1)} %constant.8.clone.t_high, bf16[2048,256]{1,0:T(8,128)(2,1)} %constant.9.clone.t_low), custom_call_target="tpu_custom_call" | custom-call | tf_op jit(solution)/shard_map/exchange/pallas_call | solution.py:417
  43.4 17.1 %finish.1 = (f32[4,8,4,2048]{3,2,1,0:T(4,128)}, f32[8,4,2048]{2,1,0:T(4,128)}) custom-call(f32[5,4,8,2048]{3,2,1,0:T(8,128)} %get-tuple-element.4.part, f32[128,128]{1,0:T(8,128)} %get-tuple-element.5.spec, bf16[256,2048]{1,0:T(8,128)(2,1)} %constant.10.clone.t_high, bf16[256,2048]{1,0:T(8,128)(2,1)} %constant.11.clone.t_low), custom_call_target="tpu_custom_call" | custom-call | tf_op jit(solution)/shard_map/finish/pallas_call | solution.py:451

commit v3 on v2

--- a/solution.py
+++ b/solution.py
@@ -346,7 +346,7 @@
     out_spec.wait()
 
 
-def finish_kernel(part, spec, t_high, t_low, new_state, potential, Y, D, M, TH, TL, PT, OUT, sem):
+def finish_kernel(part, spec, t_high, t_low, new_state, potential, Y, D, M, N, TH, TL, PT, OUT, sem):
     row = lax.axis_index("row")
     load_y = pltpu.make_async_copy(spec, Y, sem.at[8])
     load_y.start()
@@ -360,15 +360,10 @@
     load_d.start()
     load_m = pltpu.make_async_copy(part.at[pl.ds(1, 2)], M, sem.at[3])
     load_m.start()
-    plain = []
+    load_n = []
     for i, k in enumerate((0, 3)):
-        for r in range(8):
-            plain.append(
-                pltpu.make_async_copy(
-                    part.at[k, r // 2, pl.ds(4 * (r % 2), 4)], new_state.at[k, r], sem.at[4 + i]
-                )
-            )
-            plain[-1].start()
+        load_n.append(pltpu.make_async_copy(part.at[k], N.at[i], sem.at[4 + i]))
+        load_n[-1].start()
 
     load_y.wait()
     turned = Y[...].T
@@ -388,6 +383,12 @@
 
     for r in range(8):
         pltpu.make_async_copy(PT.at[pl.ds(4 * r, 4)], potential.at[r], sem.at[6]).start()
+    for i, k in enumerate((0, 3)):
+        load_n[i].wait()
+        for r in range(8):
+            pltpu.make_async_copy(
+                N.at[i, r // 2, pl.ds(4 * (r % 2), 4)], new_state.at[k, r], sem.at[9 + i]
+            ).start()
     load_d.wait()
     load_m.wait()
     for j in range(4):
@@ -406,7 +407,7 @@
     pltpu.make_async_copy(OUT, OUT, sem.at[7]).wait()
     pltpu.make_async_copy(PT.at[pl.ds(0, 32)], PT.at[pl.ds(0, 32)], sem.at[6]).wait()
     for i in range(2):
-        pltpu.make_async_copy(M.at[0], M.at[0], sem.at[4 + i]).wait()
+        pltpu.make_async_copy(N.at[i], N.at[i], sem.at[9 + i]).wait()
 
 
 def body(state, green, vertical):
@@ -460,11 +461,12 @@
             pltpu.VMEM((ROWS, 128), F32),
             pltpu.VMEM((4, *pair), F32),
             pltpu.VMEM((2, 4, *pair), F32),
+            pltpu.VMEM((2, 4, *pair), F32),
             pltpu.VMEM((2 * MODES, NPHI), BF16),
             pltpu.VMEM((2 * MODES, NPHI), BF16),
             pltpu.VMEM((72, NPHI), F32),
             pltpu.VMEM((2, 4, *pair), F32),
-            dma((9,)),
+            dma((11,)),
         ],
         compiler_params=pltpu.CompilerParams(vmem_limit_bytes=60 << 20),
         name="finish",

time: 61 us -> 47 us (0.77)
  Pallas kernels: 59.9 us -> 45.8 us
    pallas_call x1, Pallas kernels: 17.1 us -> 3.03 us  [body(): pl.pallas_call(finish_kernel, out_shape=(jax.ShapeDtypeStruct((4, 8, 4, N...]
where the time goes in v3:
time: 47 us; the launch traced here: 46.5 us
  Pallas kernels  45.8 us (97%)
  between operations  0.64 us (1%)
    pallas_call x1, Pallas kernels, body(): pl.pallas_call(exchange_kernel, out_shape=(jax.ShapeDtypeStruct((5, 4, *p...  42.8 us
    pallas_call x1, Pallas kernels, body(): pl.pallas_call(finish_kernel, out_shape=(jax.ShapeDtypeStruct((4, 8, 4, N...  3.03 us

profile of v3, /device:TPU:1, one launch (start us, length us, event | category | flops | bytes accessed | tf_op | source)
XLA Modules:
  0.0 46.5 jit_solution(15061059100802672336)
XLA Ops:
  0.6 42.8 %exchange.1 = (f32[5,4,8,2048]{3,2,1,0:T(8,128)}, f32[128,128]{1,0:T(8,128)}) custom-call(f32[4,8,4,2048]{3,2,1,0:T(4,128)} %state.1, bf16[1024,1024]{1,0:T(8,128)(2,1)} %bitcast.1, f32[16,16]{1,0:T(8,128)} %vertical.1, bf16[2048,256]{1,0:T(8,128)(2,1)} %constant.8.clone.t_high, bf16[2048,256]{1,0:T(8,128)(2,1)} %constant.9.clone.t_low), custom_call_target="tpu_custom_call" | custom-call | tf_op jit(solution)/shard_map/exchange/pallas_call | solution.py:418
  43.4 3.0 %finish.1 = (f32[4,8,4,2048]{3,2,1,0:T(4,128)}, f32[8,4,2048]{2,1,0:T(4,128)}) custom-call(f32[5,4,8,2048]{3,2,1,0:T(8,128)} %get-tuple-element.4.part, f32[128,128]{1,0:T(8,128)} %get-tuple-element.5.spec, bf16[256,2048]{1,0:T(8,128)(2,1)} %constant.10.clone.t_high, bf16[256,2048]{1,0:T(8,128)(2,1)} %constant.11.clone.t_low), custom_call_target="tpu_custom_call" | custom-call | tf_op jit(solution)/shard_map/finish/pallas_call | solution.py:452
